TPU v7x, 32 devices: a whole 2x2x4 slice. The times are simulated.
32 devices in a mesh: fsdp: 8 (over y, x, core), dp: 4 (over z).
Axes of the slice: x: 2, y: 2, z: 4, core: 2. Of those that a mesh axis runs over, the one named last changes fastest.
Arguments:
- hidden: bfloat16 [6144, 8192], P('fsdp', 'dp'), may hold values from -6 to 6
- combine_weight: float32 [6144], P('fsdp'), may hold values from 0.2 to 1
- down_weight: bfloat16 [4096, 2, 8192], P('fsdp', None, 'dp'), may hold values from -0.0625 to 0.0625
- cotangent: bfloat16 [6144, 4096], P('fsdp', 'dp'), may hold values from -6 to 6
- expert_rows: int32 [8, 2], P('fsdp'), may hold values from 1 to 640, as said below
- block_expert: int32 [48], P('fsdp'), may hold values from 0 to 1, as said below
- slot_token: int32 [6144], P('fsdp'), may hold values from 0 to 767, as said below
Outputs:
- expert_out: bfloat16 [6144, 4096], P('fsdp', 'dp')
- grad_hidden: bfloat16 [6144, 8192], P('fsdp', 'dp')
- grad_down: bfloat16 [4096, 2, 8192], P('fsdp', None, 'dp')
Inputs may be any that keep to these rules, and one draw needn't show every extreme that they name: `expert_rows`: row i gives the live rows of the first and the second expert in group i; the first expert's rows fill blocks from block 0 on, the second's start at the next free block, each takes ceil(rows / 128) blocks and both together at most 6; in every draw some group uses all 6 blocks. `block_expert`: within each group: 0 for the first expert's blocks, 1 for every later block; blocks past both experts' have no live rows. `slot_token`: tokens counted within the slot's group; the live slots of one expert in a group name different tokens of that group; slots that are not live hold arbitrary tokens.
All inputs are finite; a program needn't handle non-finite values.
Results may differ from a plain program's by a relative error of at most 0.014.
Values may be sent and summed in bfloat16 or wider, within the bound.
A program may use at most 192 MiB of HBM per device.

v0:
```python
import math

import jax
import jax.numpy as jnp
from jax import lax
from jax.sharding import PartitionSpec as P

EXPERTS = 2
BLK = 128


def local(hidden, combine_weight, down_weight, cotangent, expert_rows, block_expert, slot_token):
    slot_count = hidden.shape[0]
    hidden_width = hidden.shape[1]
    block_count = block_expert.shape[0]
    positions = jnp.arange(slot_count, dtype=jnp.int32)
    blocks = positions // BLK
    live_rows = expert_rows[0]
    first_blocks = (live_rows[0] + BLK - 1) // BLK
    second_blocks = (live_rows[1] + BLK - 1) // BLK
    live = jnp.where(
        blocks < first_blocks,
        positions < live_rows[0],
        (blocks < first_blocks + second_blocks) & (positions - first_blocks * BLK < live_rows[1]),
    )
    slot_scale = combine_weight * live.astype(jnp.float32)
    full_cot = lax.all_gather(cotangent, "dp", axis=1, tiled=True)
    model_width = full_cot.shape[1]
    slot_cot = (slot_scale[:, None] * full_cot[slot_token].astype(jnp.float32)).astype(jnp.bfloat16)
    hid_blocks = hidden.reshape(block_count, BLK, hidden_width)
    cot_blocks = slot_cot.reshape(block_count, BLK, model_width)
    panel = lax.all_gather(down_weight, "fsdp", axis=0, tiled=True)
    extent = panel.shape[0]

    def per_block(carry, inputs):
        hid_block, cot_block, expert = inputs
        weight = lax.dynamic_index_in_dim(panel, expert, 1, keepdims=False)
        out_block = jnp.einsum("th,ch->tc", hid_block, weight, preferred_element_type=jnp.float32)
        grad_block = jnp.einsum("tc,ch->th", cot_block, weight, preferred_element_type=jnp.float32)
        return (carry, (out_block, grad_block))

    unused, (out_piece, grad_piece) = lax.scan(per_block, 0, (hid_blocks, cot_blocks, block_expert))
    slot_out = out_piece.reshape(slot_count, extent)
    slot_out, hidden_grad = (slot_out, grad_piece.reshape(slot_count, hidden_width))
    token_count = cotangent.shape[0]
    combined = (
        jnp.zeros((token_count, model_width), jnp.float32)
        .at[slot_token]
        .add(slot_scale[:, None] * slot_out)
    )
    expert_out = lax.psum_scatter(
        combined.astype(jnp.bfloat16), "dp", scatter_dimension=1, tiled=True
    )
    block_marks = (block_expert[:, None] == jnp.arange(EXPERTS, dtype=jnp.int32)[None, :]).astype(
        jnp.bfloat16
    )
    slot_marks = jnp.repeat(block_marks, BLK, axis=0)
    masked = slot_marks[:, :, None] * slot_cot[:, None, :]
    summed = lax.psum_scatter(
        jnp.einsum("sec,sh->ceh", masked, hidden, preferred_element_type=jnp.float32).astype(
            jnp.bfloat16
        ),
        "fsdp",
        scatter_dimension=0,
        tiled=True,
    ).astype(jnp.float32)
    grad_scale = 1.0 / math.sqrt(lax.axis_size("fsdp") * slot_count)
    grad_down = (summed * grad_scale).astype(jnp.bfloat16)
    return (expert_out, hidden_grad.astype(jnp.bfloat16), grad_down)


def solution(mesh):
    in_specs = (
        P("fsdp", "dp"),
        P("fsdp"),
        P("fsdp", None, "dp"),
        P("fsdp", "dp"),
        P("fsdp", None),
        P("fsdp"),
        P("fsdp"),
    )
    out_specs = (P("fsdp", "dp"), P("fsdp", "dp"), P("fsdp", None, "dp"))
    return jax.shard_map(local, mesh=mesh, in_specs=in_specs, out_specs=out_specs, check_vma=False)
```

profile of v0, /device:TPU:0, one launch (start us, length us, event | category | flops | bytes accessed | tf_op | source)
XLA Modules:
  0.0 817.1 jit_solution(10564699078666156379)
XLA Ops:
  7.3 0.7 all-gather.5.cloned.1.call-update
  8.0 6.1 copy.12
  14.1 0.7 fusion.38
  16.9 1.3 fusion.39
  18.2 1.3 fusion.35
  19.6 108.1 %all-gather.5.cloned.1.call-done = bf16[768,4096]{1,0:T(8,128)(2,1)} async-done(((bf16[768,1024]{1,0:T(8,128)(2,1)}), bf16[768,4096]{1,0:T(8,128)(2,1)}) %all-gather.5.cloned.1.call-update) | async-done | bytes 6291472 | tf_op jit(solution)/shard_map/all_gather | solution.py:27
  127.7 16.1 %gather_fusion = bf16[768,4096]{1,0:T(8,128)(2,1)} fusion(bf16[768,4096]{1,0:T(8,128)(2,1)} %all-gather.5.cloned.1.call-done, s32[1024]{0:T(1024)S(1)} %pad_clamp_fusion), kind=kCustom, calls=%fused_computation | custom fusion | bytes 12585984 | tf_op jit(solution)/shard_map/gather | solution.py:29
  143.8 7.9 multiply_convert_fusion.1
  151.7 137.5 %all-gather.3.cloned.1.call-done = bf16[4096,2,2048]{2,0,1:T(8,128)(2,1)} async-done(((bf16[512,2,2048]{2,0,1:T(8,128)(2,1)}), bf16[4096,2,2048]{2,0,1:T(8,128)(2,1)}) %all-gather.3.cloned.1.call-update) | async-done | bytes 33554448 | tf_op jit(solution)/shard_map/all_gather | solution.py:32
  289.2 146.9 %while.12 = (s32[]{:T(128)}, f32[6,128,4096]{2,1,0:T(8,128)}, bf16[6,128,2048]{2,1,0:T(8,128)(2,1)}, bf16[6,128,2048]{2,1,0:T(8,128)(2,1)S(1)}, s32[6]{0:T(128)S...) while((s32[]{:T(128)}, f32[6,128,4096]{2,1,0:T(8,128)}, ...), condition=%wide.region_1.2_spmd, body=%wide.region_0.1_spmd.sunk | while | flops 4294967296 | bytes 38275224 | solution.py:42
  289.2 0.6 dynamic_slice.49
  291.7 12.7 %fusion.50 = f32[6,128,4096]{2,1,0:T(8,128)} fusion(f32[6,128,4096]{2,1,0:T(8,128)} %get-tuple-element.121, s32[]{:T(128)} %get-tuple-element.120, bf16[4096,2,2048]{2,0,1:T(8,128)(2,1)} %get-tuple-element.135, s32[]{:T(128)S(6)} %select_n.50, bf16[6,128,2048]{2,1,0:T(8,128)(2,1)S(1)} %get-tuple-element.133), kind=kOutput, calls=%fused_computation.9.clone.1 | convolution fusion | flops 2147483648 | bytes 19399684 | tf_op jit(solution)/shard_map/while/body/eval_jaxpr/th,ch->tc/dot_general | solution.py:38
  304.4 9.2 %fusion.51 = bf16[6,128,2048]{2,1,0:T(8,128)(2,1)} fusion(bf16[6,128,2048]{2,1,0:T(8,128)(2,1)} %get-tuple-element.122, s32[]{:T(128)} %get-tuple-element.120, bf16[4096,2,2048]{2,0,1:T(8,128)(2,1)} %get-tuple-element.135, s32[]{:T(128)S(6)} %select_n.50, bf16[6,128,4096]{2,1,0:T(8,128)(2,1)} %get-tuple-element.136), kind=kOutput, calls=%fused_computation.11.clone.1 | convolution fusion | flops 2147483648 | bytes 18875396 | tf_op jit(solution)/shard_map/while/body/eval_jaxpr/tc,ch->th/dot_general | solution.py:39
  316.2 12.8 %fusion.50 = f32[6,128,4096]{2,1,0:T(8,128)} fusion(f32[6,128,4096]{2,1,0:T(8,128)} %get-tuple-element.121, s32[]{:T(128)} %get-tuple-element.120, bf16[4096,2,2048]{2,0,1:T(8,128)(2,1)} %get-tuple-element.135, s32[]{:T(128)S(6)} %select_n.50, bf16[6,128,2048]{2,1,0:T(8,128)(2,1)S(1)} %get-tuple-element.133), kind=kOutput, calls=%fused_computation.9.clone.1 | convolution fusion | flops 2147483648 | bytes 19399684 | tf_op jit(solution)/shard_map/while/body/eval_jaxpr/th,ch->tc/dot_general | solution.py:38
  329.0 9.2 %fusion.51 = bf16[6,128,2048]{2,1,0:T(8,128)(2,1)} fusion(bf16[6,128,2048]{2,1,0:T(8,128)(2,1)} %get-tuple-element.122, s32[]{:T(128)} %get-tuple-element.120, bf16[4096,2,2048]{2,0,1:T(8,128)(2,1)} %get-tuple-element.135, s32[]{:T(128)S(6)} %select_n.50, bf16[6,128,4096]{2,1,0:T(8,128)(2,1)} %get-tuple-element.136), kind=kOutput, calls=%fused_computation.11.clone.1 | convolution fusion | flops 2147483648 | bytes 18875396 | tf_op jit(solution)/shard_map/while/body/eval_jaxpr/tc,ch->th/dot_general | solution.py:39
  340.7 12.7 %fusion.50 = f32[6,128,4096]{2,1,0:T(8,128)} fusion(f32[6,128,4096]{2,1,0:T(8,128)} %get-tuple-element.121, s32[]{:T(128)} %get-tuple-element.120, bf16[4096,2,2048]{2,0,1:T(8,128)(2,1)} %get-tuple-element.135, s32[]{:T(128)S(6)} %select_n.50, bf16[6,128,2048]{2,1,0:T(8,128)(2,1)S(1)} %get-tuple-element.133), kind=kOutput, calls=%fused_computation.9.clone.1 | convolution fusion | flops 2147483648 | bytes 19399684 | tf_op jit(solution)/shard_map/while/body/eval_jaxpr/th,ch->tc/dot_general | solution.py:38
  353.4 9.2 %fusion.51 = bf16[6,128,2048]{2,1,0:T(8,128)(2,1)} fusion(bf16[6,128,2048]{2,1,0:T(8,128)(2,1)} %get-tuple-element.122, s32[]{:T(128)} %get-tuple-element.120, bf16[4096,2,2048]{2,0,1:T(8,128)(2,1)} %get-tuple-element.135, s32[]{:T(128)S(6)} %select_n.50, bf16[6,128,4096]{2,1,0:T(8,128)(2,1)} %get-tuple-element.136), kind=kOutput, calls=%fused_computation.11.clone.1 | convolution fusion | flops 2147483648 | bytes 18875396 | tf_op jit(solution)/shard_map/while/body/eval_jaxpr/tc,ch->th/dot_general | solution.py:39
  365.2 12.7 %fusion.50 = f32[6,128,4096]{2,1,0:T(8,128)} fusion(f32[6,128,4096]{2,1,0:T(8,128)} %get-tuple-element.121, s32[]{:T(128)} %get-tuple-element.120, bf16[4096,2,2048]{2,0,1:T(8,128)(2,1)} %get-tuple-element.135, s32[]{:T(128)S(6)} %select_n.50, bf16[6,128,2048]{2,1,0:T(8,128)(2,1)S(1)} %get-tuple-element.133), kind=kOutput, calls=%fused_computation.9.clone.1 | convolution fusion | flops 2147483648 | bytes 19399684 | tf_op jit(solution)/shard_map/while/body/eval_jaxpr/th,ch->tc/dot_general | solution.py:38
  377.9 9.2 %fusion.51 = bf16[6,128,2048]{2,1,0:T(8,128)(2,1)} fusion(bf16[6,128,2048]{2,1,0:T(8,128)(2,1)} %get-tuple-element.122, s32[]{:T(128)} %get-tuple-element.120, bf16[4096,2,2048]{2,0,1:T(8,128)(2,1)} %get-tuple-element.135, s32[]{:T(128)S(6)} %select_n.50, bf16[6,128,4096]{2,1,0:T(8,128)(2,1)} %get-tuple-element.136), kind=kOutput, calls=%fused_computation.11.clone.1 | convolution fusion | flops 2147483648 | bytes 18875396 | tf_op jit(solution)/shard_map/while/body/eval_jaxpr/tc,ch->th/dot_general | solution.py:39
  389.7 12.8 %fusion.50 = f32[6,128,4096]{2,1,0:T(8,128)} fusion(f32[6,128,4096]{2,1,0:T(8,128)} %get-tuple-element.121, s32[]{:T(128)} %get-tuple-element.120, bf16[4096,2,2048]{2,0,1:T(8,128)(2,1)} %get-tuple-element.135, s32[]{:T(128)S(6)} %select_n.50, bf16[6,128,2048]{2,1,0:T(8,128)(2,1)S(1)} %get-tuple-element.133), kind=kOutput, calls=%fused_computation.9.clone.1 | convolution fusion | flops 2147483648 | bytes 19399684 | tf_op jit(solution)/shard_map/while/body/eval_jaxpr/th,ch->tc/dot_general | solution.py:38
  402.4 9.2 %fusion.51 = bf16[6,128,2048]{2,1,0:T(8,128)(2,1)} fusion(bf16[6,128,2048]{2,1,0:T(8,128)(2,1)} %get-tuple-element.122, s32[]{:T(128)} %get-tuple-element.120, bf16[4096,2,2048]{2,0,1:T(8,128)(2,1)} %get-tuple-element.135, s32[]{:T(128)S(6)} %select_n.50, bf16[6,128,4096]{2,1,0:T(8,128)(2,1)} %get-tuple-element.136), kind=kOutput, calls=%fused_computation.11.clone.1 | convolution fusion | flops 2147483648 | bytes 18875396 | tf_op jit(solution)/shard_map/while/body/eval_jaxpr/tc,ch->th/dot_general | solution.py:39
  414.2 12.7 %fusion.50 = f32[6,128,4096]{2,1,0:T(8,128)} fusion(f32[6,128,4096]{2,1,0:T(8,128)} %get-tuple-element.121, s32[]{:T(128)} %get-tuple-element.120, bf16[4096,2,2048]{2,0,1:T(8,128)(2,1)} %get-tuple-element.135, s32[]{:T(128)S(6)} %select_n.50, bf16[6,128,2048]{2,1,0:T(8,128)(2,1)S(1)} %get-tuple-element.133), kind=kOutput, calls=%fused_computation.9.clone.1 | convolution fusion | flops 2147483648 | bytes 19399684 | tf_op jit(solution)/shard_map/while/body/eval_jaxpr/th,ch->tc/dot_general | solution.py:38
  426.9 9.2 %fusion.51 = bf16[6,128,2048]{2,1,0:T(8,128)(2,1)} fusion(bf16[6,128,2048]{2,1,0:T(8,128)(2,1)} %get-tuple-element.122, s32[]{:T(128)} %get-tuple-element.120, bf16[4096,2,2048]{2,0,1:T(8,128)(2,1)} %get-tuple-element.135, s32[]{:T(128)S(6)} %select_n.50, bf16[6,128,4096]{2,1,0:T(8,128)(2,1)} %get-tuple-element.136), kind=kOutput, calls=%fused_computation.11.clone.1 | convolution fusion | flops 2147483648 | bytes 18875396 | tf_op jit(solution)/shard_map/while/body/eval_jaxpr/tc,ch->th/dot_general | solution.py:39
  436.1 14.9 %multiply_convert_fusion = (bf16[768,4096]{1,0:T(8,128)(2,1)}, f32[768,4096]{1,0:T(8,128)}) fusion(f32[768]{0:T(1024)S(1)} %fusion.35, bf16[768,4096]{1,0:T(8,128)(2,1)} %gather_fusion, f32[6,128,4096]{2,1,0:T(8,128)} %get-tuple-element.41), kind=kLoop, calls=%fused_computation.21 | loop fusion | flops 12582912 | bytes 37751808 | tf_op jit(solution)/shard_map/convert_element_type | solution.py:29
  451.1 8.6 %copy.13 = bf16[768,4096]{0,1:T(8,128)(2,1)} copy(bf16[768,4096]{1,0:T(8,128)(2,1)} %get-tuple-element.63) | data formatting | bytes 12582912 | tf_op jit(solution)/shard_map/convert_element_type | solution.py:29
  459.7 31.5 %convert_bitcast_fusion = bf16[4096,2,2048]{2,0,1:T(8,128)(2,1)} fusion(bf16[768,4096]{0,1:T(8,128)(2,1)} %copy.13, bf16[768,2]{0,1:T(2,128)(2,1)S(1)} %bitcast.67, bf16[768,2048]{1,0:T(8,128)(2,1)S(1)} %bitcast.66), kind=kOutput, calls=%fused_computation.18 | convolution fusion | flops 25792872448 | bytes 42994688 | tf_op jit(solution)/shard_map/sec,sh->ceh/dot_general | solution.py:60
  491.3 34.7 %scatter_custom_fusion = f32[768,4096]{1,0:T(8,128)} fusion(s32[768]{0:T(1024)} %copy-done.2, f32[768,4096]{1,0:T(8,128)} %get-tuple-element.64, f32[]{:T(128)} %constant.60.clone.1), kind=kCustom, calls=%fused_computation.26 | custom fusion | flops 3145728 | bytes 12583424 | tf_op jit(solution)/shard_map/scatter-add | solution.py:49
  526.0 11.1 %convert_element_type.51 = bf16[768,4096]{1,0:T(8,128)(2,1)} convert(f32[768,4096]{1,0:T(8,128)} %scatter_custom_fusion) | non-fusion elementwise | flops 3145728 | bytes 18874368 | tf_op jit(solution)/shard_map/convert_element_type | solution.py:52
  537.2 159.5 %reduce-scatter.5.cloned.1.call-done = bf16[512,2,2048]{2,0,1:T(8,128)(2,1)} async-done(((bf16[4096,2,2048]{2,0,1:T(8,128)(2,1)}), bf16[512,2,2048]{2,0,1:T(8,128)(2,1)}) %reduce-scatter.5.cloned.1.call-update) | async-done | bytes 4194320 | tf_op jit(solution)/shard_map/reduce_scatter | solution.py:59
  696.7 3.3 multiply_convert_fusion.2
  700.0 6.9 copy.14
  706.9 103.4 %reduce-scatter.3.cloned.1.call-done = bf16[768,1024]{1,0:T(8,128)(2,1)} async-done(((bf16[768,4096]{1,0:T(8,128)(2,1)}), bf16[768,1024]{1,0:T(8,128)(2,1)}) %reduce-scatter.3.cloned.1.call-update) | async-done | bytes 1572880 | tf_op jit(solution)/shard_map/reduce_scatter | solution.py:51
  (31 shorter events, 3.8 us)
Async XLA Ops:
  7.2 7.0 copy-start.4
  7.2 9.0 %copy-start.5 = (s32[6]{0:T(128)S(1)}, s32[6]{0:T(128)}, u32[]{:S(2)}) copy-start(s32[6]{0:T(128)} %param.14) | copy-start | bytes 76
  7.2 9.1 %copy-start.3 = (s32[768]{0:T(1024)S(1)}, s32[768]{0:T(1024)}, u32[]{:S(2)}) copy-start(s32[768]{0:T(1024)} %param.15) | copy-start | bytes 9220
  7.2 9.7 %copy-start.1 = (f32[768]{0:T(1024)S(1)}, f32[768]{0:T(1024)}, u32[]{:S(2)}) copy-start(f32[768]{0:T(1024)} %param.10) | copy-start | bytes 9220
  7.2 120.5 %all-gather.5.cloned.1.call-start = ((), (), s32[]{:S(2)}) async-start(), calls=%async_computation.3 | async-start | bytes 7864320 | tf_op jit(solution)/shard_map/all_gather | solution.py:27
  7.9 281.3 %all-gather.3.cloned.1.call-start = ((), (), s32[]{:S(2)}) async-start(), calls=%async_computation.2 | async-start | bytes 37748736 | tf_op jit(solution)/shard_map/all_gather | solution.py:32
  14.1 682.6 %reduce-scatter.5.cloned.1.call-start = ((), (), s32[]{:S(2)}) async-start(), calls=%async_computation.5 | async-start | bytes 37748736 | tf_op jit(solution)/shard_map/reduce_scatter | solution.py:59
  16.3 0.6 copy-start.2
  143.8 145.4 %copy-start = (bf16[768,2048]{1,0:T(8,128)(2,1)S(1)}, bf16[768,2048]{1,0:T(8,128)(2,1)}, u32[]{:S(2)}) copy-start(bf16[768,2048]{1,0:T(8,128)(2,1)} %param.9) | copy-start | bytes 9437188
  491.3 319.0 %reduce-scatter.3.cloned.1.call-start = ((), (), s32[]{:S(2)}) async-start(), calls=%async_computation.4 | async-start | bytes 7864320 | tf_op jit(solution)/shard_map/reduce_scatter | solution.py:51
Sparse Core Ops, SparseCore 0:
  9.6 118.0 all-gather.4
  130.2 158.9 all-gather.2
  491.4 205.2 reduce-scatter.4
  699.5 110.7 reduce-scatter.2
where the time goes:
time: 821 us; the launch traced here: 817 us
  waiting for transfers between devices  509 us (62%)
  matrix products  163 us (20%)
  other arithmetic  74.6 us (9%)
  local copies, waits for them, and re-layouts  42.5 us (5%)
  between operations  15.5 us (2%)
  loops' own time  11.7 us (1%)
    reduce_scatter x1, waiting for transfers between devices, local(): lax.psum_scatter(jnp.einsum('sec,sh->ceh', masked, hidden, preferred_elem...  160 us
    all_gather x1, waiting for transfers between devices, local(): panel = lax.all_gather(down_weight, 'fsdp', axis=0, tiled=True)  137 us
    all_gather x1, waiting for transfers between devices, local(): full_cot = lax.all_gather(cotangent, 'dp', axis=1, tiled=True)  108 us
    reduce_scatter x1, waiting for transfers between devices, local(): lax.psum_scatter(combined.astype(jnp.bfloat16), 'dp', scatter_dimension=1...  103 us
    dot_general x6, matrix products, per_block(): jnp.einsum('th,ch->tc', hid_block, weight, preferred_element_type=jnp.flo...  76.4 us
    dot_general x6, matrix products, per_block(): jnp.einsum('tc,ch->th', cot_block, weight, preferred_element_type=jnp.flo...  55.4 us
    scatter-add x1, other arithmetic, local(): combined = jnp.zeros((token_count, model_width), jnp.float32).at[slot_tok...  34.7 us
    dot_general x1, matrix products, local(): jnp.einsum('sec,sh->ceh', masked, hidden, preferred_element_type=jnp.floa...  31.5 us
  transfers between devices with their start and end apart: 4, of which 4 were waited for; matrix products, arithmetic and copies ran while one was open for 11% of the time, Pallas kernels for 0%

commit v1 on v0

v1 whole, which is shorter than its diff:
```python
import functools
import math

import jax
import jax.numpy as jnp
from jax import lax
from jax.experimental import pallas as pl
from jax.experimental.pallas import tpu as pltpu
from jax.sharding import PartitionSpec as P

EXPERTS = 2
BLK = 128
VMEM_LIMIT = 48 * 1024 * 1024


def line_gather(x, axis):
    n = lax.axis_size(axis)
    me = lax.axis_index(axis)
    right, left = [x], [x]
    for s in range(1, n):
        right.append(lax.ppermute(right[-1], axis, [(i, i + 1) for i in range(s - 1, n - 1)]))
        left.append(lax.ppermute(left[-1], axis, [(i, i - 1) for i in range(1, n - s + 1)]))
    buf = jnp.zeros((n,) + x.shape, x.dtype)
    for s in range(n):
        piece = x if s == 0 else jnp.where(me >= s, right[s], left[n - s])
        buf = lax.dynamic_update_index_in_dim(buf, piece, lax.rem(me - s + n, n), 0)
    return buf


def line_scatter(parts, axis):
    n = lax.axis_size(axis)
    me = lax.axis_index(axis)

    def term(j):
        return lax.dynamic_index_in_dim(parts, lax.rem(j + n, n), 0, keepdims=False).astype(jnp.float32)

    total = term(me)
    from_left = from_right = None
    for s in range(1, n):
        up, down = term(me + n - s), term(me - n + s)
        if from_left is not None:
            up, down = up + from_left.astype(jnp.float32), down + from_right.astype(jnp.float32)
        from_left = lax.ppermute(up.astype(parts.dtype), axis, [(i, i + 1) for i in range(s)])
        from_right = lax.ppermute(
            down.astype(parts.dtype), axis, [(i, i - 1) for i in range(n - s, n)]
        )
    if from_left is not None:
        total = total + from_left.astype(jnp.float32) + from_right.astype(jnp.float32)
    return total.astype(parts.dtype)


def slot_cot_kernel(tok_ref, scale_ref, cot_ref, out_ref):
    slots, tokens = tok_ref.shape[0], cot_ref.shape[1]
    pick = tok_ref[...] == lax.broadcasted_iota(jnp.int32, (slots, tokens), 1)
    pick = pick.astype(jnp.float32).astype(jnp.bfloat16)
    rows = jnp.dot(pick, cot_ref[0], preferred_element_type=jnp.float32)
    out_ref[...] = (scale_ref[...] * rows).astype(jnp.bfloat16)


def make_slot_cot(slot_token, slot_scale, cot_slabs):
    n, tokens, width = cot_slabs.shape
    slots = slot_token.shape[0]
    return pl.pallas_call(
        slot_cot_kernel,
        grid=(n,),
        in_specs=[
            pl.BlockSpec((slots, 1), lambda j: (0, 0)),
            pl.BlockSpec((slots, 1), lambda j: (0, 0)),
            pl.BlockSpec((1, tokens, width), lambda j: (j, 0, 0)),
        ],
        out_specs=pl.BlockSpec((slots, width), lambda j: (0, j)),
        out_shape=jax.ShapeDtypeStruct((slots, n * width), jnp.bfloat16),
        compiler_params=pltpu.CompilerParams(vmem_limit_bytes=VMEM_LIMIT),
        cost_estimate=pl.CostEstimate(
            flops=2 * slots * tokens * n * width, bytes_accessed=4 * slots * n * width, transcendentals=0
        ),
        name="slot_cot",
    )(slot_token[:, None], slot_scale[:, None], cot_slabs)


def grouped(expert_ref, w_ref, blocks, one):
    start = 0
    while start < blocks:
        first = expert_ref[start]
        if start + 1 < blocks:
            second = expert_ref[start + 1]
            both = first == second

            @pl.when(both)
            def _():
                one(start * BLK, 2 * BLK, w_ref[first])

            @pl.when(jnp.logical_not(both))
            def _():
                one(start * BLK, BLK, w_ref[first])
                one((start + 1) * BLK, BLK, w_ref[second])

            start += 2
        else:
            one(start * BLK, BLK, w_ref[first])
            start += 1


def forward_kernel(blocks, expert_ref, tok_ref, scale_ref, hid_ref, w_ref, out_ref, scaled):
    def one(row, count, w):
        rows = pl.ds(row, count)
        out = lax.dot_general(
            hid_ref[rows, :], w, (((1,), (1,)), ((), ())), preferred_element_type=jnp.float32
        )
        scaled[rows, :] = (scale_ref[rows, :] * out).astype(jnp.bfloat16)

    grouped(expert_ref, w_ref, blocks, one)
    tokens, slots = out_ref.shape[1], tok_ref.shape[1]
    put = tok_ref[...] == lax.broadcasted_iota(jnp.int32, (tokens, slots), 0)
    put = put.astype(jnp.float32).astype(jnp.bfloat16)
    out_ref[0] = jnp.dot(put, scaled[...], preferred_element_type=jnp.float32).astype(jnp.bfloat16)


def forward(block_expert, slot_token, slot_scale, hidden, panel, tokens, n):
    slots, width = hidden.shape
    model = panel.shape[1]
    part = model // n
    tile = min(512, part)
    per = part // tile
    return pl.pallas_call(
        functools.partial(forward_kernel, slots // BLK),
        grid_spec=pltpu.PrefetchScalarGridSpec(
            num_scalar_prefetch=1,
            grid=(model // tile,),
            in_specs=[
                pl.BlockSpec((1, slots), lambda d, e: (0, 0)),
                pl.BlockSpec((slots, 1), lambda d, e: (0, 0)),
                pl.BlockSpec((slots, width), lambda d, e: (0, 0)),
                pl.BlockSpec((EXPERTS, tile, width), lambda d, e: (0, d, 0)),
            ],
            out_specs=pl.BlockSpec((1, tokens, tile), lambda d, e: (d // per, 0, d % per)),
            scratch_shapes=[pltpu.VMEM((slots, tile), jnp.bfloat16)],
        ),
        out_shape=jax.ShapeDtypeStruct((n, tokens, part), jnp.bfloat16),
        compiler_params=pltpu.CompilerParams(vmem_limit_bytes=VMEM_LIMIT),
        cost_estimate=pl.CostEstimate(
            flops=2 * slots * model * (width + tokens),
            bytes_accessed=2 * EXPERTS * model * width,
            transcendentals=0,
        ),
        name="expert_forward",
    )(block_expert, slot_token[None, :], slot_scale[:, None], hidden, panel)


def hidden_grad_kernel(blocks, expert_ref, cot_ref, w_ref, out_ref):
    def one(row, count, w):
        rows = pl.ds(row, count)
        out_ref[rows, :] = jnp.dot(
            cot_ref[rows, :], w, preferred_element_type=jnp.float32
        ).astype(jnp.bfloat16)

    grouped(expert_ref, w_ref, blocks, one)


def hidden_grad(block_expert, slot_cot, panel):
    slots, model = slot_cot.shape
    width = panel.shape[2]
    tile = min(256, width)
    return pl.pallas_call(
        functools.partial(hidden_grad_kernel, slots // BLK),
        grid_spec=pltpu.PrefetchScalarGridSpec(
            num_scalar_prefetch=1,
            grid=(width // tile,),
            in_specs=[
                pl.BlockSpec((slots, model), lambda h, e: (0, 0)),
                pl.BlockSpec((EXPERTS, model, tile), lambda h, e: (0, 0, h)),
            ],
            out_specs=pl.BlockSpec((slots, tile), lambda h, e: (0, h)),
        ),
        out_shape=jax.ShapeDtypeStruct((slots, width), jnp.bfloat16),
        compiler_params=pltpu.CompilerParams(vmem_limit_bytes=VMEM_LIMIT),
        cost_estimate=pl.CostEstimate(
            flops=2 * slots * model * width,
            bytes_accessed=2 * EXPERTS * model * width,
            transcendentals=0,
        ),
        name="hidden_grad",
    )(block_expert, slot_cot, panel)


def weight_grad_kernel(blocks, first_ref, cot_ref, hid_ref, out_ref):
    width = hid_ref.shape[1]
    step = min(512, width)

    def one(expert, lo, hi, col):
        out_ref[expert, :, col : col + step] = lax.dot_general(
            cot_ref[lo:hi, :],
            hid_ref[lo:hi, col : col + step],
            (((0,), (0,)), ((), ())),
            preferred_element_type=jnp.float32,
        ).astype(jnp.bfloat16)

    for count in range(1, blocks):

        @pl.when(first_ref[0] == count)
        def _():
            for col in range(0, width, step):
                one(0, 0, count * BLK, col)
                one(1, count * BLK, blocks * BLK, col)


def weight_grad(block_expert, slot_cot, hidden):
    slots, model = slot_cot.shape
    width = hidden.shape[1]
    tile = min(512, model)
    first_blocks = jnp.sum((block_expert == 0).astype(jnp.int32)).reshape(1)
    return pl.pallas_call(
        functools.partial(weight_grad_kernel, slots // BLK),
        grid_spec=pltpu.PrefetchScalarGridSpec(
            num_scalar_prefetch=1,
            grid=(model // tile,),
            in_specs=[
                pl.BlockSpec((slots, tile), lambda d, e: (0, d)),
                pl.BlockSpec((slots, width), lambda d, e: (0, 0)),
            ],
            out_specs=pl.BlockSpec((EXPERTS, tile, width), lambda d, e: (0, d, 0)),
        ),
        out_shape=jax.ShapeDtypeStruct((EXPERTS, model, width), jnp.bfloat16),
        compiler_params=pltpu.CompilerParams(vmem_limit_bytes=VMEM_LIMIT),
        cost_estimate=pl.CostEstimate(
            flops=2 * slots * model * width,
            bytes_accessed=2 * EXPERTS * model * width,
            transcendentals=0,
        ),
        name="weight_grad",
    )(first_blocks, slot_cot, hidden)


def local(hidden, combine_weight, down_weight, cotangent, expert_rows, block_expert, slot_token):
    slot_count = hidden.shape[0]
    token_count = cotangent.shape[0]
    n = lax.axis_size("dp")
    positions = jnp.arange(slot_count, dtype=jnp.int32)
    blocks = positions // BLK
    live_rows = expert_rows[0]
    first_blocks = (live_rows[0] + BLK - 1) // BLK
    second_blocks = (live_rows[1] + BLK - 1) // BLK
    live = jnp.where(
        blocks < first_blocks,
        positions < live_rows[0],
        (blocks < first_blocks + second_blocks) & (positions - first_blocks * BLK < live_rows[1]),
    )
    slot_scale = combine_weight * live.astype(jnp.float32)
    panel = lax.all_gather(jnp.swapaxes(down_weight, 0, 1), "fsdp", axis=1, tiled=True)
    cot_slabs = line_gather(cotangent, "dp")
    slot_cot = make_slot_cot(slot_token, slot_scale, cot_slabs)
    parts = weight_grad(block_expert, slot_cot, hidden)
    sums = lax.psum_scatter(parts, "fsdp", scatter_dimension=1, tiled=True)
    token_parts = forward(block_expert, slot_token, slot_scale, hidden, panel, token_count, n)
    expert_out = line_scatter(token_parts, "dp")
    grad_hidden = hidden_grad(block_expert, slot_cot, panel)
    expert_out, grad_hidden, sums = lax.optimization_barrier((expert_out, grad_hidden, sums))
    grad_scale = 1.0 / math.sqrt(lax.axis_size("fsdp") * slot_count)
    grad_down = (jnp.swapaxes(sums, 0, 1).astype(jnp.float32) * grad_scale).astype(jnp.bfloat16)
    return (expert_out, grad_hidden, grad_down)


def solution(mesh):
    in_specs = (
        P("fsdp", "dp"),
        P("fsdp"),
        P("fsdp", None, "dp"),
        P("fsdp", "dp"),
        P("fsdp", None),
        P("fsdp"),
        P("fsdp"),
    )
    out_specs = (P("fsdp", "dp"), P("fsdp", "dp"), P("fsdp", None, "dp"))
    return jax.shard_map(local, mesh=mesh, in_specs=in_specs, out_specs=out_specs, check_vma=False)
```

time: 821 us -> 403 us (0.49)
  waiting for transfers between devices: 509 us -> 219 us
  matrix products: 163 us -> 0 us
  Pallas kernels: 0 us -> 92 us
  other arithmetic: 74.6 us -> 22.7 us
  starting transfers between devices: 0.16 us -> 31.8 us
  local copies, waits for them, and re-layouts: 42.5 us -> 21.5 us
  loops' own time: 11.7 us -> 0 us
    reduce_scatter x2 -> x1, waiting for transfers between devices: 263 us -> 10.2 us  [local(): sums = lax.psum_scatter(parts, 'fsdp', scatter_dimension=1, tiled=True)]
    all_gather x2 -> x1, waiting for transfers between devices: 246 us -> 8.13 us  [local(): lax.all_gather(jnp.swapaxes(down_weight, 0, 1), 'fsdp', axis=1, tiled=True)]
    ppermute x0 -> x12, waiting for transfers between devices: none -> 200 us  [the longest x3 95.2 us: line_gather(): lax.ppermute(left[-1], axis, [(i, i - 1) for i in range(1, n - s + 1)])]
    dot_general x13 -> x0, matrix products: 163 us -> none  [the longest x6 76.4 us: per_block(): jnp.einsum('th,ch->tc', hid_block, weight, preferred_element_type=jnp.flo...]
    pallas_call x0 -> x4, Pallas kernels: none -> 92 us  [the longest x1 34.5 us: forward(): pl.pallas_call(functools.partial(forward_kernel, slots // BLK), grid_spec...]
    scatter-add x1 -> x0, other arithmetic: 34.7 us -> none  [local(): combined = jnp.zeros((token_count, model_width), jnp.float32).at[slot_tok...]
    ppermute x0 -> x12, starting transfers between devices: none -> 31.8 us  [the longest x3 14.7 us: line_scatter(): lax.ppermute(up.astype(parts.dtype), axis, [(i, i + 1) for i in range(s)])]
    convert_element_type x5, other arithmetic: 37.3 us -> 15 us  [the longest x2 8.73 us: line_scatter(): up.astype(parts.dtype)]
  transfers between devices with their start and end apart: 4 -> 14, of which waited for: 4 -> 9; matrix products, arithmetic and copies ran while one was open for 11% -> 6% of each run, Pallas kernels for 0% -> 23%
where the time goes in v1:
time: 403 us; the launch traced here: 402 us
  waiting for transfers between devices  219 us (54%)
  Pallas kernels  92 us (23%)
  starting transfers between devices  31.8 us (8%)
  other arithmetic  22.7 us (6%)
  local copies, waits for them, and re-layouts  21.5 us (5%)
  between operations  15.6 us (4%)
    ppermute x3, waiting for transfers between devices, line_gather(): lax.ppermute(left[-1], axis, [(i, i - 1) for i in range(1, n - s + 1)])  95.2 us
    ppermute x3, waiting for transfers between devices, line_scatter(): lax.ppermute(up.astype(parts.dtype), axis, [(i, i + 1) for i in range(s)])  69 us
    ppermute x3, waiting for transfers between devices, line_scatter(): lax.ppermute(down.astype(parts.dtype), axis, [(i, i - 1) for i in range(n...  36.2 us
    pallas_call x1, Pallas kernels, forward(): pl.pallas_call(functools.partial(forward_kernel, slots // BLK), grid_spec...  34.5 us
    pallas_call x1, Pallas kernels, hidden_grad(): pl.pallas_call(functools.partial(hidden_grad_kernel, slots // BLK), grid_...  24.8 us
    pallas_call x1, Pallas kernels, weight_grad(): pl.pallas_call(functools.partial(weight_grad_kernel, slots // BLK), grid_...  23.5 us
    unnamed x26, local copies, waits for them, and re-layouts  15.6 us
    ppermute x3, starting transfers between devices, line_scatter(): lax.ppermute(up.astype(parts.dtype), axis, [(i, i + 1) for i in range(s)])  14.7 us
  transfers between devices with their start and end apart: 14, of which 9 were waited for; matrix products, arithmetic and copies ran while one was open for 6% of the time, Pallas kernels for 23%

profile of v1, /device:TPU:0, one launch (start us, length us, event | category | flops | bytes accessed | tf_op | source)
XLA Modules:
  0.0 402.3 jit_solution(10555737972933256771)
XLA Ops:
  7.2 6.1 %copy.18 = bf16[512,2,2048]{2,0,1:T(8,128)(2,1)} copy(bf16[512,2,2048]{2,1,0:T(2,128)(2,1)} %param.9) | data formatting | bytes 8388608 | tf_op args[2]
  13.4 1.3 collective-permute-start.7
  14.7 5.7 %collective-permute-start.6 = (bf16[768,1024]{1,0:T(8,128)(2,1)}, bf16[768,1024]{1,0:T(8,128)(2,1)S(1)}, u32[]{:S(2)}, u32[]{:S(2)}) collective-permute-start(bf16[768,1024]{1,0:T(8,128)(2,1)} %param.10), channel_id=1, source_target_pairs={{0,1},{1,2},{2,3},{4,5},{5,6},{6,7},{8,9},{9,10},{10,11},{12,13},{... | collective-permute-start | bytes 4718600 | tf_op jit(solution)/shard_map/ppermute | solution.py:21
  20.3 32.6 %collective-permute-done.7 = bf16[768,1024]{1,0:T(8,128)(2,1)S(1)} collective-permute-done((bf16[768,1024]{1,0:T(8,128)(2,1)}, bf16[768,1024]{1,0:T(8,128)(2,1)S(1)}, u32[]{:S(2)}, u32[]{:S(2)}) %collective-permute-start.7) | collective-permute-done | bytes 1572896 | tf_op jit(solution)/shard_map/ppermute | solution.py:22
  54.2 1.8 collective-permute-start.10
  56.0 34.5 %collective-permute-done.8 = bf16[768,1024]{1,0:T(8,128)(2,1)} collective-permute-done((bf16[768,1024]{1,0:T(8,128)(2,1)S(1)}, bf16[768,1024]{1,0:T(8,128)(2,1)}, u32[]{:S(2)}, u32[]{:S(2)}) %collective-permute-start.8) | collective-permute-done | bytes 1572896 | tf_op jit(solution)/shard_map/ppermute | solution.py:22
  91.9 1.9 collective-permute-start.11
  99.4 28.1 %collective-permute-done.9 = bf16[768,1024]{1,0:T(8,128)(2,1)} collective-permute-done((bf16[768,1024]{1,0:T(8,128)(2,1)}, bf16[768,1024]{1,0:T(8,128)(2,1)}, u32[]{:S(2)}, u32[]{:S(2)}) %collective-permute-start.9) | collective-permute-done | bytes 1572896 | tf_op jit(solution)/shard_map/ppermute | solution.py:22
  127.5 2.4 bitcast_dynamic-update-slice_fusion.2
  130.0 2.4 bitcast_dynamic-update-slice_fusion.1
  133.5 2.6 copy-done.3
  136.1 9.3 %slot_cot.1.cot_ref = bf16[768,4096]{1,0:T(8,128)(2,1)} custom-call(s32[768,1]{1,0:T(8,128)S(1)} %broadcast_in_dim.35.tok_ref, f32[768,1]{1,0:T(8,128)S(1)} %broadcast_in_dim.34.scale_ref, bf16[4,768,1024]{2,1,0:T(8,128)(2,1)} %copy-done.3), custom_call_target="tpu_custom_call" | custom-call | flops 4831838208 | bytes 12582912 | tf_op jit(solution)/shard_map/slot_cot/pallas_call | solution.py:63
  145.3 23.5 %weight_grad.1 = bf16[2,4096,2048]{2,1,0:T(8,128)(2,1)} custom-call(s32[1]{0:T(128)} %bitcast.14.first_ref, bf16[768,4096]{1,0:T(8,128)(2,1)} %slot_cot.1.cot_ref, bf16[768,2048]{1,0:T(8,128)(2,1)S(1)} %copy-done), custom_call_target="tpu_custom_call" | custom-call | flops 12884901888 | bytes 33554432 | tf_op jit(solution)/shard_map/weight_grad/pallas_call | solution.py:212
  168.8 8.1 %all-gather.2.cloned.1.call-done.w_ref = bf16[2,4096,2048]{2,1,0:T(8,128)(2,1)} async-done(((bf16[2,512,2048]{2,1,0:T(8,128)(2,1)}), bf16[2,4096,2048]{2,1,0:T(8,128)(2,1)}) %all-gather.2.cloned.1.call-update) | async-done | bytes 33554448 | tf_op jit(solution)/shard_map/all_gather | solution.py:249
  177.0 34.5 %expert_forward.1 = bf16[4,768,1024]{2,1,0:T(8,128)(2,1)} custom-call(s32[6]{0:T(128)S(1)} %copy-done.2, s32[1,768]{1,0:T(1,128)S(1)} %broadcast_in_dim.26.tok_ref, f32[768,1]{1,0:T(8,128)S(1)} %broadcast_in_dim.34.scale_ref, bf16[768,2048]{1,0:T(8,128)(2,1)S(1)} %copy-done.1, bf16[2,4096,2048]{2,1,0:T(8,128)(2,1)} %all-gather.2.cloned.1.call-done.w_ref), custom_call_target="tpu_custom_call" | custom-call | flops 17716740096 | bytes 33554432 | tf_op jit(solution)/shard_map/expert_forward/pallas_call | solution.py:125
  211.5 4.0 dynamic-slice_bitcast_fusion.1
  215.4 4.5 %collective-permute-start = (bf16[768,1024]{1,0:T(8,128)(2,1)S(1)}, bf16[768,1024]{1,0:T(8,128)(2,1)}, u32[]{:S(2)}, u32[]{:S(2)}) collective-permute-start(bf16[768,1024]{1,0:T(8,128)(2,1)S(1)} %get-tuple-element.17), channel_id=1, source_target_pairs={{0,1},{4,5},{8,9},{12,13},{16,17},{20,21},{24,25},{28,29}} | collective-permute-start | bytes 4718600 | tf_op jit(solution)/shard_map/ppermute | solution.py:43
  219.9 1.8 collective-permute-start.3
  221.7 31.0 %collective-permute-done = bf16[768,1024]{1,0:T(8,128)(2,1)} collective-permute-done((bf16[768,1024]{1,0:T(8,128)(2,1)S(1)}, bf16[768,1024]{1,0:T(8,128)(2,1)}, u32[]{:S(2)}, u32[]{:S(2)}) %collective-permute-start) | collective-permute-done | bytes 1572896 | tf_op jit(solution)/shard_map/ppermute | solution.py:43
  252.8 4.0 %fusion.3 = bf16[768,1024]{1,0:T(8,128)(2,1)} fusion(bf16[768,1024]{1,0:T(8,128)(2,1)} %collective-permute-done, bf16[4,768,1024]{2,1,0:T(8,128)(2,1)} %expert_forward.1, s32[]{:T(128)S(6)} %select_n.72), kind=kLoop, calls=%fused_computation.8 | loop fusion | flops 3145728 | bytes 4718596 | tf_op jit(solution)/shard_map/convert_element_type | solution.py:43
  256.8 5.5 %collective-permute-start.1 = (bf16[768,1024]{1,0:T(8,128)(2,1)}, bf16[768,1024]{1,0:T(8,128)(2,1)}, u32[]{:S(2)}, u32[]{:S(2)}) collective-permute-start(bf16[768,1024]{1,0:T(8,128)(2,1)} %fusion.3), channel_id=1, source_target_pairs={{0,1},{1,2},{4,5},{5,6},{8,9},{9,10},{12,13},{13,14},{16,17},{17,1... | collective-permute-start | bytes 4718600 | tf_op jit(solution)/shard_map/ppermute | solution.py:43
  262.3 32.3 %collective-permute-done.1 = bf16[768,1024]{1,0:T(8,128)(2,1)} collective-permute-done((bf16[768,1024]{1,0:T(8,128)(2,1)}, bf16[768,1024]{1,0:T(8,128)(2,1)}, u32[]{:S(2)}, u32[]{:S(2)}) %collective-permute-start.1) | collective-permute-done | bytes 1572896 | tf_op jit(solution)/shard_map/ppermute | solution.py:43
  294.6 4.7 %fusion.4 = (bf16[768,1024]{1,0:T(8,128)(2,1)S(1)}, bf16[768,1024]{1,0:T(8,128)(2,1)S(1)}) fusion(bf16[768,1024]{1,0:T(8,128)(2,1)} %collective-permute-done.1, bf16[4,768,1024]{2,1,0:T(8,128)(2,1)} %expert_forward.1, s32[]{:T(128)S(6)} %select_n.71, bf16[768,1024]{1,0:T(8,128)(2,1)} %collective-permute-done.3, s32[]{:T(128)S(6)} %select_n.75), kind=kLoop, calls=%fused_computation.10 | loop fusion | flops 6291456 | bytes 9437192 | tf_op jit(solution)/shard_map/convert_element_type | solution.py:43
  300.1 4.8 %collective-permute-start.2 = (bf16[768,1024]{1,0:T(8,128)(2,1)S(1)}, bf16[768,1024]{1,0:T(8,128)(2,1)S(1)}, u32[]{:S(2)}, u32[]{:S(2)}) collective-permute-start(bf16[768,1024]{1,0:T(8,128)(2,1)S(1)} %get-tuple-element.15), channel_id=1, source_target_pairs={{0,1},{1,2},{2,3},{4,5},{5,6},{6,7},{8,9},{9,10},{10,11},{12,13},{... | collective-permute-start | bytes 4718600 | tf_op jit(solution)/shard_map/ppermute | solution.py:43
  305.6 1.3 collective-permute-start.5
  306.9 24.8 %hidden_grad.1 = bf16[768,2048]{1,0:T(8,128)(2,1)} custom-call(s32[6]{0:T(128)S(1)} %copy-done.2, bf16[768,4096]{1,0:T(8,128)(2,1)} %slot_cot.1.cot_ref, bf16[2,4096,2048]{2,1,0:T(8,128)(2,1)} %all-gather.2.cloned.1.call-done.w_ref), custom_call_target="tpu_custom_call" | custom-call | flops 12884901888 | bytes 33554432 | tf_op jit(solution)/shard_map/hidden_grad/pallas_call | solution.py:164
  331.7 5.6 %collective-permute-done.2 = bf16[768,1024]{1,0:T(8,128)(2,1)S(1)} collective-permute-done((bf16[768,1024]{1,0:T(8,128)(2,1)S(1)}, bf16[768,1024]{1,0:T(8,128)(2,1)S(1)}, u32[]{:S(2)}, u32[]{:S(2)}) %collective-permute-start.2) | collective-permute-done | bytes 1572896 | tf_op jit(solution)/shard_map/ppermute | solution.py:43
  337.3 36.2 %collective-permute-done.5 = bf16[768,1024]{1,0:T(8,128)(2,1)S(1)} collective-permute-done((bf16[768,1024]{1,0:T(8,128)(2,1)S(1)}, bf16[768,1024]{1,0:T(8,128)(2,1)S(1)}, u32[]{:S(2)}, u32[]{:S(2)}) %collective-permute-start.5) | collective-permute-done | bytes 1572896 | tf_op jit(solution)/shard_map/ppermute | solution.py:44
  373.4 2.2 fusion.6
  375.7 10.2 %reduce-scatter.2.cloned.1.call-done = bf16[2,512,2048]{2,1,0:T(8,128)(2,1)} async-done(((bf16[2,4096,2048]{2,1,0:T(8,128)(2,1)}), bf16[2,512,2048]{2,1,0:T(8,128)(2,1)}) %reduce-scatter.2.cloned.1.call-update) | async-done | bytes 4194320 | tf_op jit(solution)/shard_map/reduce_scatter | solution.py:253
  385.8 3.3 fusion
  389.1 6.3 %copy.16 = bf16[512,2,2048]{2,1,0:T(2,128)(2,1)} copy(bf16[512,2,2048]{2,0,1:T(8,128)(2,1)S(1)} %fusion) | data formatting | bytes 8388608
  (46 shorter events, 9.6 us)
Async XLA Ops:
  7.2 169.8 %all-gather.2.cloned.1.call-start = ((), (), s32[]{:S(2)}) async-start(), calls=%async_computation.1 | async-start | bytes 37748736 | tf_op jit(solution)/shard_map/all_gather | solution.py:249
  13.3 80.5 %copy-start.9 = (s32[1,2]{1,0:T(1,128)S(1)}, s32[1,2]{1,0:T(1,128)}, u32[]{:S(2)}) copy-start(s32[1,2]{1,0:T(1,128)} %param.11) | copy-start | bytes 28
  13.3 82.3 %copy-start.8 = (f32[768]{0:T(1024)S(1)}, f32[768]{0:T(1024)}, u32[]{:S(2)}) copy-start(f32[768]{0:T(1024)} %param.8) | copy-start | bytes 9220
  13.3 83.7 %copy-start.7 = (s32[768]{0:T(1024)S(1)}, s32[768]{0:T(1024)}, u32[]{:S(2)}) copy-start(s32[768]{0:T(1024)} %param.13) | copy-start | bytes 9220
  13.3 83.9 %copy-start.2 = (s32[6]{0:T(128)S(1)}, s32[6]{0:T(128)}, u32[]{:S(2)}) copy-start(s32[6]{0:T(128)} %expert_ref.3) | copy-start | bytes 76
  13.3 372.5 %reduce-scatter.2.cloned.1.call-start = ((), (), s32[]{:S(2)}) async-start(), calls=%async_computation.2 | async-start | bytes 37748736 | tf_op jit(solution)/shard_map/reduce_scatter | solution.py:253
  13.4 39.5 %collective-permute-start.7 = (bf16[768,1024]{1,0:T(8,128)(2,1)}, bf16[768,1024]{1,0:T(8,128)(2,1)S(1)}, u32[]{:S(2)}, u32[]{:S(2)}) collective-permute-start(bf16[768,1024]{1,0:T(8,128)(2,1)} %param.10), channel_id=1, source_target_pairs={{1,0},{2,1},{3,2},{5,4},{6,5},{7,6},{9,8},{10,9},{11,10},{13,12},{... | collective-permute-start | bytes 4718600 | tf_op jit(solution)/shard_map/ppermute | solution.py:22
  14.7 39.5 %collective-permute-start.6 = (bf16[768,1024]{1,0:T(8,128)(2,1)}, bf16[768,1024]{1,0:T(8,128)(2,1)S(1)}, u32[]{:S(2)}, u32[]{:S(2)}) collective-permute-start(bf16[768,1024]{1,0:T(8,128)(2,1)} %param.10), channel_id=1, source_target_pairs={{0,1},{1,2},{2,3},{4,5},{5,6},{6,7},{8,9},{9,10},{10,11},{12,13},{... | collective-permute-start | bytes 4718600 | tf_op jit(solution)/shard_map/ppermute | solution.py:21
  52.9 37.7 %collective-permute-start.8 = (bf16[768,1024]{1,0:T(8,128)(2,1)S(1)}, bf16[768,1024]{1,0:T(8,128)(2,1)}, u32[]{:S(2)}, u32[]{:S(2)}) collective-permute-start(bf16[768,1024]{1,0:T(8,128)(2,1)S(1)} %collective-permute-done.7), channel_id=1, source_target_pairs={{1,0},{2,1},{5,4},{6,5},{9,8},{10,9},{13,12},{14,13},{17,16},{18,1... | collective-permute-start | bytes 4718600 | tf_op jit(solution)/shard_map/ppermute | solution.py:22
  54.2 36.4 %copy-start.4 = (bf16[768,1024]{1,0:T(8,128)(2,1)}, bf16[768,1024]{1,0:T(8,128)(2,1)S(1)}, u32[]{:S(2)}) copy-start(bf16[768,1024]{1,0:T(8,128)(2,1)S(1)} %collective-permute-done.6) | copy-start | bytes 4718596
  54.2 37.7 %collective-permute-start.10 = (bf16[768,1024]{1,0:T(8,128)(2,1)S(1)}, bf16[768,1024]{1,0:T(8,128)(2,1)}, u32[]{:S(2)}, u32[]{:S(2)}) collective-permute-start(bf16[768,1024]{1,0:T(8,128)(2,1)S(1)} %collective-permute-done.6), channel_id=1, source_target_pairs={{1,2},{2,3},{5,6},{6,7},{9,10},{10,11},{13,14},{14,15},{17,18},{18... | collective-permute-start | bytes 4718600 | tf_op jit(solution)/shard_map/ppermute | solution.py:21
  90.6 37.0 %collective-permute-start.9 = (bf16[768,1024]{1,0:T(8,128)(2,1)}, bf16[768,1024]{1,0:T(8,128)(2,1)}, u32[]{:S(2)}, u32[]{:S(2)}) collective-permute-start(bf16[768,1024]{1,0:T(8,128)(2,1)} %collective-permute-done.8), channel_id=1, source_target_pairs={{1,0},{5,4},{9,8},{13,12},{17,16},{21,20},{25,24},{29,28}} | collective-permute-start | bytes 4718600 | tf_op jit(solution)/shard_map/ppermute | solution.py:22
  91.9 40.5 %collective-permute-start.11 = (bf16[768,1024]{1,0:T(8,128)(2,1)}, bf16[768,1024]{1,0:T(8,128)(2,1)}, u32[]{:S(2)}, u32[]{:S(2)}) collective-permute-start(bf16[768,1024]{1,0:T(8,128)(2,1)} %collective-permute-done.10), channel_id=1, source_target_pairs={{2,3},{6,7},{10,11},{14,15},{18,19},{22,23},{26,27},{30,31}} | collective-permute-start | bytes 4718600 | tf_op jit(solution)/shard_map/ppermute | solution.py:21
  97.8 1.4 copy-start.6
  99.2 28.3 %copy-start.5 = (bf16[768,1024]{1,0:T(8,128)(2,1)S(1)}, bf16[768,1024]{1,0:T(8,128)(2,1)}, u32[]{:S(2)}) copy-start(bf16[768,1024]{1,0:T(8,128)(2,1)} %copy-done.4) | copy-start | bytes 4718596
  133.4 2.6 copy-start.3
  136.0 9.3 %copy-start = (bf16[768,2048]{1,0:T(8,128)(2,1)S(1)}, bf16[768,2048]{1,0:T(8,128)(2,1)}, u32[]{:S(2)}) copy-start(bf16[768,2048]{1,0:T(8,128)(2,1)} %hid_ref.3) | copy-start | bytes 9437188
  168.8 8.2 %copy-start.1 = (bf16[768,2048]{1,0:T(8,128)(2,1)S(1)}, bf16[768,2048]{1,0:T(8,128)(2,1)}, u32[]{:S(2)}) copy-start(bf16[768,2048]{1,0:T(8,128)(2,1)} %hid_ref.3) | copy-start | bytes 9437188
  215.4 37.3 %collective-permute-start = (bf16[768,1024]{1,0:T(8,128)(2,1)S(1)}, bf16[768,1024]{1,0:T(8,128)(2,1)}, u32[]{:S(2)}, u32[]{:S(2)}) collective-permute-start(bf16[768,1024]{1,0:T(8,128)(2,1)S(1)} %get-tuple-element.17), channel_id=1, source_target_pairs={{0,1},{4,5},{8,9},{12,13},{16,17},{20,21},{24,25},{28,29}} | collective-permute-start | bytes 4718600 | tf_op jit(solution)/shard_map/ppermute | solution.py:43
  219.9 42.4 %collective-permute-start.3 = (bf16[768,1024]{1,0:T(8,128)(2,1)}, bf16[768,1024]{1,0:T(8,128)(2,1)}, u32[]{:S(2)}, u32[]{:S(2)}) collective-permute-start(bf16[768,1024]{1,0:T(8,128)(2,1)} %get-tuple-element.18), channel_id=1, source_target_pairs={{3,2},{7,6},{11,10},{15,14},{19,18},{23,22},{27,26},{31,30}} | collective-permute-start | bytes 4718600 | tf_op jit(solution)/shard_map/ppermute | solution.py:44
  252.8 52.1 %slice-start = ((s8[6291456]{0:T(1024)(128)(4,1)}), s8[2097152]{0:T(1024)(128)(4,1)S(1)}, s32[]{:S(2)}) async-start(s8[6291456]{0:T(1024)(128)(4,1)} %bitcast.35), calls=%async_computation.3 | async-start | bytes 4194304
  256.8 37.8 %collective-permute-start.1 = (bf16[768,1024]{1,0:T(8,128)(2,1)}, bf16[768,1024]{1,0:T(8,128)(2,1)}, u32[]{:S(2)}, u32[]{:S(2)}) collective-permute-start(bf16[768,1024]{1,0:T(8,128)(2,1)} %fusion.3), channel_id=1, source_target_pairs={{0,1},{1,2},{4,5},{5,6},{8,9},{9,10},{12,13},{13,14},{16,17},{17,1... | collective-permute-start | bytes 4718600 | tf_op jit(solution)/shard_map/ppermute | solution.py:43
  262.3 42.6 %slice-start.1 = ((s8[6291456]{0:T(1024)(128)(4,1)}), s8[4194304]{0:T(1024)(128)(4,1)S(1)}, s32[]{:S(2)}) async-start(s8[6291456]{0:T(1024)(128)(4,1)} %bitcast.35), calls=%async_computation.4 | async-start | bytes 8388608
  299.3 5.5 %collective-permute-start.4 = (bf16[768,1024]{1,0:T(8,128)(2,1)S(1)}, bf16[768,1024]{1,0:T(8,128)(2,1)S(1)}, u32[]{:S(2)}, u32[]{:S(2)}) collective-permute-start(bf16[768,1024]{1,0:T(8,128)(2,1)S(1)} %get-tuple-element.16), channel_id=1, source_target_pairs={{2,1},{3,2},{6,5},{7,6},{10,9},{11,10},{14,13},{15,14},{18,17},{19... | collective-permute-start | bytes 4718600 | tf_op jit(solution)/shard_map/ppermute | solution.py:44
  300.1 37.2 %collective-permute-start.2 = (bf16[768,1024]{1,0:T(8,128)(2,1)S(1)}, bf16[768,1024]{1,0:T(8,128)(2,1)S(1)}, u32[]{:S(2)}, u32[]{:S(2)}) collective-permute-start(bf16[768,1024]{1,0:T(8,128)(2,1)S(1)} %get-tuple-element.15), channel_id=1, source_target_pairs={{0,1},{1,2},{2,3},{4,5},{5,6},{6,7},{8,9},{9,10},{10,11},{12,13},{... | collective-permute-start | bytes 4718600 | tf_op jit(solution)/shard_map/ppermute | solution.py:43
  305.6 67.8 %collective-permute-start.5 = (bf16[768,1024]{1,0:T(8,128)(2,1)S(1)}, bf16[768,1024]{1,0:T(8,128)(2,1)S(1)}, u32[]{:S(2)}, u32[]{:S(2)}) collective-permute-start(bf16[768,1024]{1,0:T(8,128)(2,1)S(1)} %fusion.2), channel_id=1, source_target_pairs={{1,0},{2,1},{3,2},{5,4},{6,5},{7,6},{9,8},{10,9},{11,10},{13,12},{... | collective-permute-start | bytes 4718600 | tf_op jit(solution)/shard_map/ppermute | solution.py:44
Sparse Core Ops, SparseCore 0:
  13.4 163.4 all-gather.1
  180.5 205.2 reduce-scatter.1
